TPU v7x, 32 devices: a whole 2x2x4 slice. The times are simulated.
32 devices in a mesh: dir: 2 (over x), gx: 16 (over z, y, core).
Axes of the slice: x: 2, y: 2, z: 4, core: 2. Of those that a mesh axis runs over, the one named last changes fastest.
Arguments:
- pops: float32 [19, 128, 64, 128], P(None, ('dir', 'gx')), parts along dimension 1, may hold values from 0.5 to 1.5
- heights: int32 [128, 128], P(('dir', 'gx')), parts along dimension 0, may hold values from 0 to 32
Outputs:
- pops_out: float32 [19, 128, 64, 128], P(None, ('dir', 'gx')), parts along dimension 1
There are 2 independent parts, one for each index of `dir`. A program takes and returns all parts, laid end to end along the dimension named above; each array names one. Nothing has to cross between parts.
All inputs are finite; a program needn't handle non-finite values.
Results may differ from a plain program's by a relative error of at most 0.0003.
Values sent between devices are 32-bit elements; how exact they have to be, the bound alone decides.
A program may use at most 64 MiB of HBM per device.

v0:
```python
import functools

import jax
import jax.numpy as jnp
from jax import lax
from jax.experimental import pallas as pl
from jax.experimental.pallas import tpu as pltpu
from jax.sharding import PartitionSpec as P

STEPS = 6
PAD = 8
MESH = pl.DeviceIdType.MESH

velocity_table = [
    (0, 0, 0),
    (1, 0, 0),
    (-1, 0, 0),
    (0, 1, 0),
    (0, -1, 0),
    (0, 0, 1),
    (0, 0, -1),
    (1, 1, 0),
    (-1, -1, 0),
    (1, -1, 0),
    (-1, 1, 0),
    (1, 0, 1),
    (-1, 0, -1),
    (1, 0, -1),
    (-1, 0, 1),
    (0, 1, 1),
    (0, -1, -1),
    (0, 1, -1),
    (0, -1, 1),
]
omega_rate = 1.9
held_order = [1, 7, 9, 11, 13, 2, 8, 10, 12, 14, 0, 3, 4, 5, 6, 15, 16, 17, 18]
spot = {component: place for place, component in enumerate(held_order)}
MOVING = 5


def opposite(component):
    if component == 0:
        return 0
    return component + 1 if component % 2 == 1 else component - 1


def collide(g):
    sums = {i: g[i] + g[i + 1] for i in range(1, 19, 2)}
    diffs = {i: g[i] - g[i + 1] for i in range(1, 19, 2)}
    axis_sum = sums[1] + sums[3] + sums[5]
    cross_sum = (sums[7] + sums[9]) + (sums[11] + sums[13]) + (sums[15] + sums[17])
    total = 12.0 * g[0] + 2.0 * axis_sum + cross_sum
    scale = 3.0 * omega_rate / 36.0
    nx = scale * (2.0 * diffs[1] + ((diffs[7] + diffs[9]) + (diffs[11] + diffs[13])))
    ny = scale * (2.0 * diffs[3] + ((diffs[7] - diffs[9]) + (diffs[15] + diffs[17])))
    nz = scale * (2.0 * diffs[5] + ((diffs[11] - diffs[13]) + (diffs[15] - diffs[17])))
    k = (omega_rate * 4.5 / 36.0 / (scale * scale)) / total
    base = (omega_rate / 36.0) * total - (k * (1.0 / 3.0)) * (nx * nx + ny * ny + nz * nz)
    along = {1: nx, 3: ny, 5: nz, 7: nx + ny, 9: nx - ny, 11: nx + nz, 13: nx - nz, 15: ny + nz, 17: ny - nz}
    keep = 1.0 - omega_rate
    post = {0: base + keep * g[0]}
    for i, t in along.items():
        even = base + k * (t * t)
        post[i] = (even + t) + keep * g[i]
        post[i + 1] = (even - t) + keep * g[i + 1]
    return post


def stream(walls, rows, depth, held, plane, first):
    lanes = held.shape[-1]
    z = lax.broadcasted_iota(jnp.int32, (rows, lanes), 0) + first
    source_z = {0: z, 1: z - 1, -1: jnp.where(z == depth - 1, -1, z + 1)}
    here = pl.ds(pl.multiple_of(PAD + first, 8), rows)
    post = {i: held[spot[i], plane, here, :] for i in range(19)}
    g = {}
    for i in range(19):
        cx, cy, cz = velocity_table[i]
        if cx == 0 and cz == 0:
            moved = post[i]
        elif cz == 0:
            moved = held[spot[i], plane - cx, here, :]
        else:
            moved = held[spot[i], plane - cx, pl.ds(PAD + first - cz, rows), :]
        if cy != 0:
            moved = pltpu.roll(moved, cy % lanes, 1)
        fluid = source_z[cz] >= walls[1 + cy, plane - cx]
        g[i] = jnp.where(fluid, moved, post[opposite(i)])
    return g


def kernel(n, rows, pops, heights, last_post, walls, stage, other_post, ground, ground_sem, in_sem, sent_up, sent_down, got_up, got_down, wall_sem):
    width, depth, lanes = pops.shape[1], pops.shape[2], pops.shape[3]
    chunks = depth // rows
    even_post, odd_post = (other_post, last_post) if STEPS % 2 == 0 else (last_post, other_post)
    me = lax.axis_index("gx")
    right, left = lax.rem(me + 1, n), lax.rem(me + n - 1, n)
    edges = [1, width] if width > 1 else [1]
    inner = list(range(2, width))

    ground_fetch = pltpu.make_async_copy(heights, ground, ground_sem)
    ground_fetch.start()
    fetches = {}
    for plane in edges + inner:
        fetches[plane] = pltpu.make_async_copy(pops.at[:, plane - 1], stage.at[:, plane - 1], in_sem.at[plane - 1])
        fetches[plane].start()

    barrier = pltpu.get_barrier_semaphore()
    for neighbour in (left, right):
        pl.semaphore_signal(barrier, inc=1, device_id={"gx": neighbour}, device_id_type=MESH)

    wall_up = pltpu.make_async_remote_copy(
        walls.at[1, width], walls.at[1, 0], wall_sem.at[0], wall_sem.at[1], device_id={"gx": right}, device_id_type=MESH)
    wall_down = pltpu.make_async_remote_copy(
        walls.at[1, 1], walls.at[1, width + 1], wall_sem.at[2], wall_sem.at[3], device_id={"gx": left}, device_id_type=MESH)

    def copies(held, step, chunk):
        span = pl.ds(pl.multiple_of(PAD + chunk * rows, 8), rows)
        up = pltpu.make_async_remote_copy(
            held.at[pl.ds(0, MOVING), width, span], held.at[pl.ds(0, MOVING), 0, span],
            sent_up.at[step, chunk], got_up.at[step, chunk], device_id={"gx": right}, device_id_type=MESH)
        down = pltpu.make_async_remote_copy(
            held.at[pl.ds(MOVING, MOVING), 1, span], held.at[pl.ds(MOVING, MOVING), width + 1, span],
            sent_down.at[step, chunk], got_down.at[step, chunk], device_id={"gx": left}, device_id_type=MESH)
        return up, down

    def arrived(held, step, chunk):
        for copy in copies(held, step, chunk):
            copy.wait_recv()

    def left_here(held, step, chunk):
        for copy in copies(held, step, chunk):
            copy.wait_send()

    def keep_post(held, first, posts):
        span = pl.ds(pl.multiple_of(PAD + first, 8), rows)
        for plane, post in posts.items():
            for i in range(19):
                held[spot[i], plane, span, :] = post[i]

    stream_here = functools.partial(stream, walls, rows, depth)

    def first_post(planes, chunk):
        first = chunk * rows
        span = pl.ds(pl.multiple_of(first, 8), rows)
        keep_post(even_post, first, {
            plane: collide({i: stage[i, plane - 1, span, :] for i in range(19)}) for plane in planes
        })

    ground_fetch.wait()
    for plane in range(1, width + 1):
        walls[1, plane] = jnp.broadcast_to(ground[plane - 1 : plane, :], (rows, lanes))
    for plane in edges:
        fetches[plane].wait()
    first_post(edges, 0)
    pl.semaphore_wait(barrier, 2)
    wall_up.start()
    wall_down.start()
    for copy in copies(even_post, 0, 0):
        copy.start()

    def first_chunk(chunk, carry):
        first_post(edges, chunk)
        for copy in copies(even_post, 0, chunk):
            copy.start()
        return carry

    lax.fori_loop(1, chunks, first_chunk, 0)
    for plane in inner:
        fetches[plane].wait()

    def first_inner(chunk, carry):
        first_post(inner, chunk)
        return carry

    lax.fori_loop(0, chunks, first_inner, 0)

    wall_up.wait()
    wall_down.wait()
    for plane in range(width + 2):
        for cy in (1, -1):
            walls[1 + cy, plane] = pltpu.roll(walls[1, plane], cy % lanes, 1)

    def one_step(step, before, held):
        arrived(before, step - 1, 0)

        def one_chunk(chunk, inside):
            first = chunk * rows

            @pl.when(chunk < chunks - 1)
            def _():
                arrived(before, step - 1, chunk + 1)

            @pl.when(step >= 2)
            def _():
                left_here(held, step - 2, chunk)

            keep_post(held, first, {plane: collide(stream_here(before, plane, first)) for plane in edges})
            for copy in copies(held, step, chunk):
                copy.start()
            keep_post(held, first, {plane: collide(stream_here(before, plane, first)) for plane in inner})
            return inside

        lax.fori_loop(0, chunks, one_chunk, 0)

    def two_steps(pair, carry):
        one_step(2 * pair + 1, even_post, odd_post)
        one_step(2 * pair + 2, odd_post, even_post)
        return carry

    lax.fori_loop(0, (STEPS - 1) // 2, two_steps, 0)
    if STEPS % 2 == 0:
        one_step(STEPS - 1, even_post, odd_post)

    def last_inner(chunk, carry):
        first = chunk * rows
        span = pl.ds(pl.multiple_of(first, 8), rows)
        streamed = {plane: stream_here(last_post, plane, first) for plane in inner}
        for plane, g in streamed.items():
            for i in range(19):
                stage[i, plane - 1, span, :] = g[i]
        return carry

    lax.fori_loop(0, chunks, last_inner, 0)

    def finish(chunk, carry):
        left_here(other_post, STEPS - 2, chunk)
        left_here(last_post, STEPS - 1, chunk)
        arrived(last_post, STEPS - 1, chunk)
        return carry

    lax.fori_loop(0, chunks, finish, 0)


def last_kernel(rows, last_post, walls, stage, out, ends, inner_sem, out_sem):
    width, depth = stage.shape[1], stage.shape[2]
    chunks = depth // rows
    edges = [1, width] if width > 1 else [1]
    inner_copies = [
        pltpu.make_async_copy(stage.at[:, plane - 1], out.at[:, plane - 1], inner_sem.at[plane - 1])
        for plane in range(2, width)
    ]
    for copy in inner_copies:
        copy.start()

    def write_back(chunk):
        span = pl.ds(pl.multiple_of(chunk * rows, 8), rows)
        return [
            pltpu.make_async_copy(ends.at[:, place, span], out.at[:, plane - 1, span], out_sem.at[chunk, place])
            for place, plane in enumerate(edges)
        ]

    def one_chunk(chunk, carry):
        first = chunk * rows
        span = pl.ds(pl.multiple_of(first, 8), rows)
        streamed = [stream(walls, rows, depth, last_post, plane, first) for plane in edges]
        for place, g in enumerate(streamed):
            for i in range(19):
                ends[i, place, span, :] = g[i]
        for copy in write_back(chunk):
            copy.start()
        return carry

    lax.fori_loop(0, chunks, one_chunk, 0)

    def finish(chunk, carry):
        for copy in write_back(chunk):
            copy.wait()
        return carry

    lax.fori_loop(0, chunks, finish, 0)
    for copy in inner_copies:
        copy.wait()


def solution(mesh):
    n = mesh.shape["gx"]

    def per_device(pops, heights):
        kinds, width, depth, lanes = pops.shape
        rows = 8
        chunks = depth // rows
        dma = pltpu.SemaphoreType.DMA
        held_shape = (kinds, width + 2, depth + 2 * PAD, lanes)
        wall_shape = (3, width + 2, rows, lanes)
        hbm, vmem = pl.BlockSpec(memory_space=pltpu.HBM), pl.BlockSpec(memory_space=pltpu.VMEM)
        kept = pl.pallas_call(
            functools.partial(kernel, n, rows),
            out_shape=[
                pltpu.VMEM(held_shape, jnp.float32),
                pltpu.VMEM(wall_shape, jnp.int32),
                pltpu.VMEM(pops.shape, jnp.float32),
            ],
            in_specs=[hbm] * 2,
            out_specs=[vmem] * 3,
            scratch_shapes=[
                pltpu.VMEM(held_shape, jnp.float32),
                pltpu.VMEM(heights.shape, jnp.int32),
                dma,
                dma((width,)),
                dma((STEPS, chunks)),
                dma((STEPS, chunks)),
                dma((STEPS, chunks)),
                dma((STEPS, chunks)),
                dma((4,)),
            ],
            compiler_params=pltpu.CompilerParams(
                collective_id=0, has_side_effects=True, vmem_limit_bytes=55 * 1024 * 1024
            ),
            cost_estimate=pl.CostEstimate(
                flops=250 * STEPS * width * depth * lanes, bytes_accessed=4 * pops.size, transcendentals=0
            ),
        )(pops, heights)
        return pl.pallas_call(
            functools.partial(last_kernel, rows),
            out_shape=jax.ShapeDtypeStruct(pops.shape, pops.dtype),
            in_specs=[vmem] * 3,
            out_specs=hbm,
            scratch_shapes=[
                pltpu.VMEM((kinds, min(width, 2), depth, lanes), jnp.float32),
                dma((width,)),
                dma((chunks, 2)),
            ],
            compiler_params=pltpu.CompilerParams(vmem_limit_bytes=32 * 1024 * 1024),
            cost_estimate=pl.CostEstimate(flops=20 * pops.size, bytes_accessed=4 * pops.size, transcendentals=0),
        )(*kept)

    return jax.shard_map(
        per_device,
        mesh=mesh,
        in_specs=(P(None, ("dir", "gx"), None, None), P(("dir", "gx"), None)),
        out_specs=P(None, ("dir", "gx"), None, None),
        check_vma=False,
    )
```

profile of v0, /device:TPU:0, one launch (start us, length us, event | category | flops | bytes accessed | tf_op | source)
XLA Modules:
  0.0 34.9 jit_solution(5706080654463779308)
XLA Ops:
  0.0 33.3 %shard_map.28 = (f32[19,6,80,128]{3,2,1,0:T(8,128)S(1)}, s32[3,6,8,128]{3,2,1,0:T(8,128)S(1)}, f32[19,4,64,128]{3,2,1,0:T(8,128)S(1)}) custom-call(f32[19,4,64,128]{3,2,1,0:T(8,128)} %pops.1, s32[4,128]{1,0:T(4,128)} %heights.1), custom_call_target="tpu_custom_call" | custom-call | flops 49152000 | bytes 2490368 | tf_op jit(solution)/shard_map/pallas_call | solution.py:286
  33.3 1.6 %shard_map.29 = f32[19,4,64,128]{3,2,1,0:T(8,128)} custom-call(f32[19,6,80,128]{3,2,1,0:T(8,128)S(1)} %get-tuple-element.8.last_post, s32[3,6,8,128]{3,2,1,0:T(8,128)S(1)} %get-tuple-element.9.walls, f32[19,4,64,128]{3,2,1,0:T(8,128)S(1)} %get-tuple-element.10.stage), custom_call_target="tpu_custom_call" | custom-call | flops 12451840 | bytes 2490368 | tf_op jit(solution)/shard_map/pallas_call | solution.py:313
where the time goes:
time: 35 us; the launch traced here: 34.9 us
  Pallas kernels  34.9 us (100%)
    pallas_call x1, Pallas kernels, per_device(): pl.pallas_call(functools.partial(kernel, n, rows), out_shape=[pltpu.VMEM(...  33.3 us
    pallas_call x1, Pallas kernels, per_device(): pl.pallas_call(functools.partial(last_kernel, rows), out_shape=jax.ShapeD...  1.61 us

commit v1 on v0

--- a/solution.py
+++ b/solution.py
@@ -88,7 +88,7 @@
     return g
 
 
-def kernel(n, rows, pops, heights, last_post, walls, stage, other_post, ground, ground_sem, in_sem, sent_up, sent_down, got_up, got_down, wall_sem):
+def kernel(n, rows, pops, heights, stage, last_post, other_post, walls, ground, ground_sem, in_sem, sent_up, sent_down, got_up, got_down, wall_sem):
     width, depth, lanes = pops.shape[1], pops.shape[2], pops.shape[3]
     chunks = depth // rows
     even_post, odd_post = (other_post, last_post) if STEPS % 2 == 0 else (last_post, other_post)
@@ -97,12 +97,14 @@
     edges = [1, width] if width > 1 else [1]
     inner = list(range(2, width))
 
+    fetches = {
+        plane: pltpu.make_async_copy(pops.at[:, plane - 1], stage.at[:, plane - 1], in_sem.at[plane - 1])
+        for plane in edges + inner
+    }
+    for plane in edges:
+        fetches[plane].start()
     ground_fetch = pltpu.make_async_copy(heights, ground, ground_sem)
     ground_fetch.start()
-    fetches = {}
-    for plane in edges + inner:
-        fetches[plane] = pltpu.make_async_copy(pops.at[:, plane - 1], stage.at[:, plane - 1], in_sem.at[plane - 1])
-        fetches[plane].start()
 
     barrier = pltpu.get_barrier_semaphore()
     for neighbour in (left, right):
@@ -146,17 +148,19 @@
             plane: collide({i: stage[i, plane - 1, span, :] for i in range(19)}) for plane in planes
         })
 
+    for plane in edges:
+        fetches[plane].wait()
+    for plane in inner:
+        fetches[plane].start()
+    first_post(edges, 0)
+    pl.semaphore_wait(barrier, 2)
+    for copy in copies(even_post, 0, 0):
+        copy.start()
     ground_fetch.wait()
     for plane in range(1, width + 1):
         walls[1, plane] = jnp.broadcast_to(ground[plane - 1 : plane, :], (rows, lanes))
-    for plane in edges:
-        fetches[plane].wait()
-    first_post(edges, 0)
-    pl.semaphore_wait(barrier, 2)
     wall_up.start()
     wall_down.start()
-    for copy in copies(even_post, 0, 0):
-        copy.start()
 
     def first_chunk(chunk, carry):
         first_post(edges, chunk)
@@ -221,54 +225,39 @@
         return carry
 
     lax.fori_loop(0, chunks, last_inner, 0)
+    arrived(last_post, STEPS - 1, 0)
+
+    def last_edges(chunk, carry):
+        first = chunk * rows
+        span = pl.ds(pl.multiple_of(first, 8), rows)
+
+        @pl.when(chunk < chunks - 1)
+        def _():
+            arrived(last_post, STEPS - 1, chunk + 1)
+
+        streamed = {plane: stream_here(last_post, plane, first) for plane in edges}
+        for plane, g in streamed.items():
+            for i in range(19):
+                stage[i, plane - 1, span, :] = g[i]
+        return carry
+
+    lax.fori_loop(0, chunks, last_edges, 0)
 
     def finish(chunk, carry):
         left_here(other_post, STEPS - 2, chunk)
         left_here(last_post, STEPS - 1, chunk)
-        arrived(last_post, STEPS - 1, chunk)
         return carry
 
     lax.fori_loop(0, chunks, finish, 0)
 
 
-def last_kernel(rows, last_post, walls, stage, out, ends, inner_sem, out_sem):
-    width, depth = stage.shape[1], stage.shape[2]
-    chunks = depth // rows
-    edges = [1, width] if width > 1 else [1]
-    inner_copies = [
-        pltpu.make_async_copy(stage.at[:, plane - 1], out.at[:, plane - 1], inner_sem.at[plane - 1])
-        for plane in range(2, width)
+def write_kernel(stage, out, sem):
+    copies = [
+        pltpu.make_async_copy(stage.at[:, plane], out.at[:, plane], sem.at[plane]) for plane in range(stage.shape[1])
     ]
-    for copy in inner_copies:
+    for copy in copies:
         copy.start()
-
-    def write_back(chunk):
-        span = pl.ds(pl.multiple_of(chunk * rows, 8), rows)
-        return [
-            pltpu.make_async_copy(ends.at[:, place, span], out.at[:, plane - 1, span], out_sem.at[chunk, place])
-            for place, plane in enumerate(edges)
-        ]
-
-    def one_chunk(chunk, carry):
-        first = chunk * rows
-        span = pl.ds(pl.multiple_of(first, 8), rows)
-        streamed = [stream(walls, rows, depth, last_post, plane, first) for plane in edges]
-        for place, g in enumerate(streamed):
-            for i in range(19):
-                ends[i, place, span, :] = g[i]
-        for copy in write_back(chunk):
-            copy.start()
-        return carry
-
-    lax.fori_loop(0, chunks, one_chunk, 0)
-
-    def finish(chunk, carry):
-        for copy in write_back(chunk):
-            copy.wait()
-        return carry
-
-    lax.fori_loop(0, chunks, finish, 0)
-    for copy in inner_copies:
+    for copy in copies:
         copy.wait()
 
 
@@ -277,7 +266,7 @@
 
     def per_device(pops, heights):
         kinds, width, depth, lanes = pops.shape
-        rows = 8
+        rows = 16 if depth % 16 == 0 else 8
         chunks = depth // rows
         dma = pltpu.SemaphoreType.DMA
         held_shape = (kinds, width + 2, depth + 2 * PAD, lanes)
@@ -285,15 +274,13 @@
         hbm, vmem = pl.BlockSpec(memory_space=pltpu.HBM), pl.BlockSpec(memory_space=pltpu.VMEM)
         kept = pl.pallas_call(
             functools.partial(kernel, n, rows),
-            out_shape=[
+            out_shape=pltpu.VMEM(pops.shape, jnp.float32),
+            in_specs=[hbm] * 2,
+            out_specs=vmem,
+            scratch_shapes=[
+                pltpu.VMEM(held_shape, jnp.float32),
                 pltpu.VMEM(held_shape, jnp.float32),
                 pltpu.VMEM(wall_shape, jnp.int32),
-                pltpu.VMEM(pops.shape, jnp.float32),
-            ],
-            in_specs=[hbm] * 2,
-            out_specs=[vmem] * 3,
-            scratch_shapes=[
-                pltpu.VMEM(held_shape, jnp.float32),
                 pltpu.VMEM(heights.shape, jnp.int32),
                 dma,
                 dma((width,)),
@@ -304,25 +291,21 @@
                 dma((4,)),
             ],
             compiler_params=pltpu.CompilerParams(
-                collective_id=0, has_side_effects=True, vmem_limit_bytes=55 * 1024 * 1024
+                collective_id=0, has_side_effects=True, vmem_limit_bytes=60 * 1024 * 1024
             ),
             cost_estimate=pl.CostEstimate(
                 flops=250 * STEPS * width * depth * lanes, bytes_accessed=4 * pops.size, transcendentals=0
             ),
         )(pops, heights)
         return pl.pallas_call(
-            functools.partial(last_kernel, rows),
-            out_shape=jax.ShapeDtypeStruct(pops.shape, pops.dtype),
-            in_specs=[vmem] * 3,
+            write_kernel,
+            out_shape=pltpu.HBM(pops.shape, jnp.float32),
+            in_specs=[vmem],
             out_specs=hbm,
-            scratch_shapes=[
-                pltpu.VMEM((kinds, min(width, 2), depth, lanes), jnp.float32),
-                dma((width,)),
-                dma((chunks, 2)),
-            ],
+            scratch_shapes=[dma((width,))],
             compiler_params=pltpu.CompilerParams(vmem_limit_bytes=32 * 1024 * 1024),
-            cost_estimate=pl.CostEstimate(flops=20 * pops.size, bytes_accessed=4 * pops.size, transcendentals=0),
-        )(*kept)
+            cost_estimate=pl.CostEstimate(flops=0, bytes_accessed=4 * pops.size, transcendentals=0),
+        )(kept)
 
     return jax.shard_map(
         per_device,

time: 35 us -> 36.4 us (1.040)
  Pallas kernels: 34.9 us -> 36.3 us
    pallas_call x2, Pallas kernels: 34.9 us -> 36.3 us  [the longest x1 34.8 us: per_device(): pl.pallas_call(functools.partial(kernel, n, rows), out_shape=pltpu.VMEM(p...]
where the time goes in v1:
time: 36.4 us; the launch traced here: 36.3 us
  Pallas kernels  36.3 us (100%)
    pallas_call x1, Pallas kernels, per_device(): pl.pallas_call(functools.partial(kernel, n, rows), out_shape=pltpu.VMEM(p...  34.8 us
    pallas_call x1, Pallas kernels, per_device(): pl.pallas_call(write_kernel, out_shape=pltpu.HBM(pops.shape, jnp.float32)...  1.48 us

profile of v1, /device:TPU:0, one launch (start us, length us, event | category | flops | bytes accessed | tf_op | source)
XLA Modules:
  0.0 36.3 jit_solution(14735483900809262034)
XLA Ops:
  0.0 34.8 %shard_map.28.stage = f32[19,4,64,128]{3,2,1,0:T(8,128)S(1)} custom-call(f32[19,4,64,128]{3,2,1,0:T(8,128)} %pops.1, s32[4,128]{1,0:T(4,128)} %heights.1), custom_call_target="tpu_custom_call" | custom-call | flops 49152000 | bytes 2490368 | tf_op jit(solution)/shard_map/pallas_call | solution.py:275
  34.8 1.5 %shard_map.29 = f32[19,4,64,128]{3,2,1,0:T(8,128)} custom-call(f32[19,4,64,128]{3,2,1,0:T(8,128)S(1)} %shard_map.28.stage), custom_call_target="tpu_custom_call" | custom-call | bytes 2490368 | tf_op jit(solution)/shard_map/pallas_call | solution.py:300

commit v2 on v0

--- a/solution.py
+++ b/solution.py
@@ -97,12 +97,14 @@
     edges = [1, width] if width > 1 else [1]
     inner = list(range(2, width))
 
+    fetches = {
+        plane: pltpu.make_async_copy(pops.at[:, plane - 1], stage.at[:, plane - 1], in_sem.at[plane - 1])
+        for plane in edges + inner
+    }
+    for plane in edges:
+        fetches[plane].start()
     ground_fetch = pltpu.make_async_copy(heights, ground, ground_sem)
     ground_fetch.start()
-    fetches = {}
-    for plane in edges + inner:
-        fetches[plane] = pltpu.make_async_copy(pops.at[:, plane - 1], stage.at[:, plane - 1], in_sem.at[plane - 1])
-        fetches[plane].start()
 
     barrier = pltpu.get_barrier_semaphore()
     for neighbour in (left, right):
@@ -146,17 +148,19 @@
             plane: collide({i: stage[i, plane - 1, span, :] for i in range(19)}) for plane in planes
         })
 
+    for plane in edges:
+        fetches[plane].wait()
+    for plane in inner:
+        fetches[plane].start()
+    first_post(edges, 0)
+    pl.semaphore_wait(barrier, 2)
+    for copy in copies(even_post, 0, 0):
+        copy.start()
     ground_fetch.wait()
     for plane in range(1, width + 1):
         walls[1, plane] = jnp.broadcast_to(ground[plane - 1 : plane, :], (rows, lanes))
-    for plane in edges:
-        fetches[plane].wait()
-    first_post(edges, 0)
-    pl.semaphore_wait(barrier, 2)
     wall_up.start()
     wall_down.start()
-    for copy in copies(even_post, 0, 0):
-        copy.start()
 
     def first_chunk(chunk, carry):
         first_post(edges, chunk)
@@ -190,14 +194,11 @@
             def _():
                 arrived(before, step - 1, chunk + 1)
 
-            @pl.when(step >= 2)
-            def _():
-                left_here(held, step - 2, chunk)
-
             keep_post(held, first, {plane: collide(stream_here(before, plane, first)) for plane in edges})
             for copy in copies(held, step, chunk):
                 copy.start()
             keep_post(held, first, {plane: collide(stream_here(before, plane, first)) for plane in inner})
+            left_here(before, step - 1, chunk)
             return inside
 
         lax.fori_loop(0, chunks, one_chunk, 0)
@@ -223,7 +224,6 @@
     lax.fori_loop(0, chunks, last_inner, 0)
 
     def finish(chunk, carry):
-        left_here(other_post, STEPS - 2, chunk)
         left_here(last_post, STEPS - 1, chunk)
         arrived(last_post, STEPS - 1, chunk)
         return carry

time: 35 us -> 35.1 us (level)
  no operation moved by 1% of the time
where the time goes in v2:
time: 35.1 us; the launch traced here: 35 us
  Pallas kernels  34.9 us (99%)
    pallas_call x1, Pallas kernels, per_device(): pl.pallas_call(functools.partial(kernel, n, rows), out_shape=[pltpu.VMEM(...  33.3 us
    pallas_call x1, Pallas kernels, per_device(): pl.pallas_call(functools.partial(last_kernel, rows), out_shape=jax.ShapeD...  1.61 us

profile of v2, /device:TPU:0, one launch (start us, length us, event | category | flops | bytes accessed | tf_op | source)
XLA Modules:
  0.0 35.0 jit_solution(16414901332220084324)
XLA Ops:
  0.0 33.3 %shard_map.28 = (f32[19,6,80,128]{3,2,1,0:T(8,128)S(1)}, s32[3,6,8,128]{3,2,1,0:T(8,128)S(1)}, f32[19,4,64,128]{3,2,1,0:T(8,128)S(1)}) custom-call(f32[19,4,64,128]{3,2,1,0:T(8,128)} %pops.1, s32[4,128]{1,0:T(4,128)} %heights.1), custom_call_target="tpu_custom_call" | custom-call | flops 49152000 | bytes 2490368 | tf_op jit(solution)/shard_map/pallas_call | solution.py:286
  33.3 1.6 %shard_map.29 = f32[19,4,64,128]{3,2,1,0:T(8,128)} custom-call(f32[19,6,80,128]{3,2,1,0:T(8,128)S(1)} %get-tuple-element.8.last_post, s32[3,6,8,128]{3,2,1,0:T(8,128)S(1)} %get-tuple-element.9.walls, f32[19,4,64,128]{3,2,1,0:T(8,128)S(1)} %get-tuple-element.10.stage), custom_call_target="tpu_custom_call" | custom-call | flops 12451840 | bytes 2490368 | tf_op jit(solution)/shard_map/pallas_call | solution.py:313

commit v3 on v2

--- a/solution.py
+++ b/solution.py
@@ -101,8 +101,8 @@
         plane: pltpu.make_async_copy(pops.at[:, plane - 1], stage.at[:, plane - 1], in_sem.at[plane - 1])
         for plane in edges + inner
     }
-    for plane in edges:
-        fetches[plane].start()
+    for place, plane in enumerate(edges):
+        fetches[plane].start(priority=place % 2)
     ground_fetch = pltpu.make_async_copy(heights, ground, ground_sem)
     ground_fetch.start()
 
@@ -150,8 +150,8 @@
 
     for plane in edges:
         fetches[plane].wait()
-    for plane in inner:
-        fetches[plane].start()
+    for place, plane in enumerate(inner):
+        fetches[plane].start(priority=place % 2)
     first_post(edges, 0)
     pl.semaphore_wait(barrier, 2)
     for copy in copies(even_post, 0, 0):
@@ -239,8 +239,8 @@
         pltpu.make_async_copy(stage.at[:, plane - 1], out.at[:, plane - 1], inner_sem.at[plane - 1])
         for plane in range(2, width)
     ]
-    for copy in inner_copies:
-        copy.start()
+    for place, copy in enumerate(inner_copies):
+        copy.start(priority=place % 2)
 
     def write_back(chunk):
         span = pl.ds(pl.multiple_of(chunk * rows, 8), rows)
@@ -256,8 +256,8 @@
         for place, g in enumerate(streamed):
             for i in range(19):
                 ends[i, place, span, :] = g[i]
-        for copy in write_back(chunk):
-            copy.start()
+        for place, copy in enumerate(write_back(chunk)):
+            copy.start(priority=place)
         return carry
 
     lax.fori_loop(0, chunks, one_chunk, 0)

time: 35.1 us -> 35.1 us (level)
  no operation moved by 1% of the time
where the time goes in v3:
time: 35.1 us; the launch traced here: 35 us
  Pallas kernels  34.9 us (99%)
    pallas_call x1, Pallas kernels, per_device(): pl.pallas_call(functools.partial(kernel, n, rows), out_shape=[pltpu.VMEM(...  33.3 us
    pallas_call x1, Pallas kernels, per_device(): pl.pallas_call(functools.partial(last_kernel, rows), out_shape=jax.ShapeD...  1.61 us

profile of v3, /device:TPU:0, one launch (start us, length us, event | category | flops | bytes accessed | tf_op | source)
XLA Modules:
  0.0 35.0 jit_solution(13138403951708021693)
XLA Ops:
  0.0 33.3 %shard_map.28 = (f32[19,6,80,128]{3,2,1,0:T(8,128)S(1)}, s32[3,6,8,128]{3,2,1,0:T(8,128)S(1)}, f32[19,4,64,128]{3,2,1,0:T(8,128)S(1)}) custom-call(f32[19,4,64,128]{3,2,1,0:T(8,128)} %pops.1, s32[4,128]{1,0:T(4,128)} %heights.1), custom_call_target="tpu_custom_call" | custom-call | flops 49152000 | bytes 2490368 | tf_op jit(solution)/shard_map/pallas_call | solution.py:286
  33.3 1.6 %shard_map.29 = f32[19,4,64,128]{3,2,1,0:T(8,128)} custom-call(f32[19,6,80,128]{3,2,1,0:T(8,128)S(1)} %get-tuple-element.8.last_post, s32[3,6,8,128]{3,2,1,0:T(8,128)S(1)} %get-tuple-element.9.walls, f32[19,4,64,128]{3,2,1,0:T(8,128)S(1)} %get-tuple-element.10.stage), custom_call_target="tpu_custom_call" | custom-call | flops 12451840 | bytes 2490368 | tf_op jit(solution)/shard_map/pallas_call | solution.py:313

commit v4 on v2

--- a/solution.py
+++ b/solution.py
@@ -36,6 +36,8 @@
 held_order = [1, 7, 9, 11, 13, 2, 8, 10, 12, 14, 0, 3, 4, 5, 6, 15, 16, 17, 18]
 spot = {component: place for place, component in enumerate(held_order)}
 MOVING = 5
+RELAY = 3
+LAG_UP, LAG_DOWN = 4, 3
 
 
 def opposite(component):
@@ -88,7 +90,7 @@
     return g
 
 
-def kernel(n, rows, pops, heights, last_post, walls, stage, other_post, ground, ground_sem, in_sem, sent_up, sent_down, got_up, got_down, wall_sem):
+def kernel(n, rows, pops, heights, last_post, walls, stage, other_post, ground, ground_sem, in_sem, sent_up, sent_down, got_up, got_down, wall_sem, *relay):
     width, depth, lanes = pops.shape[1], pops.shape[2], pops.shape[3]
     chunks = depth // rows
     even_post, odd_post = (other_post, last_post) if STEPS % 2 == 0 else (last_post, other_post)
@@ -96,6 +98,9 @@
     right, left = lax.rem(me + 1, n), lax.rem(me + n - 1, n)
     edges = [1, width] if width > 1 else [1]
     inner = list(range(2, width))
+    relayed = len(relay) > 0
+    if relayed:
+        (relay_up, relay_down, relay_got_up, relay_got_down, relay_sent_up, relay_sent_down) = relay
 
     fetches = {
         plane: pltpu.make_async_copy(pops.at[:, plane - 1], stage.at[:, plane - 1], in_sem.at[plane - 1])
@@ -109,6 +114,19 @@
     barrier = pltpu.get_barrier_semaphore()
     for neighbour in (left, right):
         pl.semaphore_signal(barrier, inc=1, device_id={"gx": neighbour}, device_id_type=MESH)
+    if relayed:
+
+        @pl.when(me == RELAY)
+        def _():
+            for end in (0, n - 1):
+                pl.semaphore_signal(barrier, inc=1, device_id={"gx": end}, device_id_type=MESH)
+
+        for end in (0, n - 1):
+
+            @pl.when(me == end)
+            def _():
+                pl.semaphore_signal(barrier, inc=1, device_id={"gx": RELAY}, device_id_type=MESH)
+
 
     wall_up = pltpu.make_async_remote_copy(
         walls.at[1, width], walls.at[1, 0], wall_sem.at[0], wall_sem.at[1], device_id={"gx": right}, device_id_type=MESH)
@@ -125,6 +143,48 @@
             sent_down.at[step, chunk], got_down.at[step, chunk], device_id={"gx": left}, device_id_type=MESH)
         return up, down
 
+    def relay_copies(held, step, chunk):
+        span = pl.ds(pl.multiple_of(PAD + chunk * rows, 8), rows)
+        part = pl.ds(pl.multiple_of(chunk * rows, 8), rows)
+        to_up = pltpu.make_async_remote_copy(
+            held.at[pl.ds(0, MOVING), width, span], relay_up.at[step, :, part],
+            sent_up.at[step, chunk], relay_got_up.at[step, chunk], device_id={"gx": RELAY}, device_id_type=MESH)
+        from_up = pltpu.make_async_remote_copy(
+            relay_up.at[step, :, part], held.at[pl.ds(0, MOVING), 0, span],
+            relay_sent_up.at[step, chunk], got_up.at[step, chunk], device_id={"gx": 0}, device_id_type=MESH)
+        to_down = pltpu.make_async_remote_copy(
+            held.at[pl.ds(MOVING, MOVING), 1, span], relay_down.at[step, :, part],
+            sent_down.at[step, chunk], relay_got_down.at[step, chunk], device_id={"gx": RELAY}, device_id_type=MESH)
+        from_down = pltpu.make_async_remote_copy(
+            relay_down.at[step, :, part], held.at[pl.ds(MOVING, MOVING), width + 1, span],
+            relay_sent_down.at[step, chunk], got_down.at[step, chunk], device_id={"gx": n - 1}, device_id_type=MESH)
+        return to_up, from_up, to_down, from_down
+
+    def send(held, step, chunk):
+        up, down = copies(held, step, chunk)
+        if not relayed:
+            up.start()
+            down.start()
+            return
+        to_up, _, to_down, _ = relay_copies(held, step, chunk)
+        for copy, to_relay, end in ((up, to_up, n - 1), (down, to_down, 0)):
+            pl.when(me != end)(copy.start)
+            pl.when(me == end)(to_relay.start)
+
+    def pass_on(held, before, step, chunk):
+        def one(buffer, its_step, its_chunk, upward):
+            to_up, from_up, to_down, from_down = relay_copies(buffer, its_step, its_chunk)
+            came, leaves = (to_up, from_up) if upward else (to_down, from_down)
+            came.wait_recv()
+            leaves.start()
+
+        for lag, upward in ((LAG_DOWN, False), (LAG_UP, True)):
+            if held is not None:
+                pl.when((me == RELAY) & (chunk >= lag))(lambda: one(held, step, chunk - lag, upward))
+            if before is not None:
+                pl.when((me == RELAY) & (chunk < lag))(
+                    lambda: one(before, step - 1, chunk + chunks - lag, upward))
+
     def arrived(held, step, chunk):
         for copy in copies(held, step, chunk):
             copy.wait_recv()
@@ -153,9 +213,17 @@
     for plane in inner:
         fetches[plane].start()
     first_post(edges, 0)
-    pl.semaphore_wait(barrier, 2)
-    for copy in copies(even_post, 0, 0):
-        copy.start()
+    if relayed:
+        at_end = (me == 0) | (me == n - 1)
+        for peers, where in ((4, me == RELAY), (3, at_end), (2, (me != RELAY) & ~at_end)):
+
+            @pl.when(where)
+            def _():
+                pl.semaphore_wait(barrier, peers)
+
+    else:
+        pl.semaphore_wait(barrier, 2)
+    send(even_post, 0, 0)
     ground_fetch.wait()
     for plane in range(1, width + 1):
         walls[1, plane] = jnp.broadcast_to(ground[plane - 1 : plane, :], (rows, lanes))
@@ -164,8 +232,7 @@
 
     def first_chunk(chunk, carry):
         first_post(edges, chunk)
-        for copy in copies(even_post, 0, chunk):
-            copy.start()
+        send(even_post, 0, chunk)
         return carry
 
     lax.fori_loop(1, chunks, first_chunk, 0)
@@ -173,6 +240,8 @@
         fetches[plane].wait()
 
     def first_inner(chunk, carry):
+        if relayed:
+            pass_on(even_post, None, 0, chunk)
         first_post(inner, chunk)
         return carry
 
@@ -195,8 +264,9 @@
                 arrived(before, step - 1, chunk + 1)
 
             keep_post(held, first, {plane: collide(stream_here(before, plane, first)) for plane in edges})
-            for copy in copies(held, step, chunk):
-                copy.start()
+            send(held, step, chunk)
+            if relayed:
+                pass_on(held, before, step, chunk)
             keep_post(held, first, {plane: collide(stream_here(before, plane, first)) for plane in inner})
             left_here(before, step - 1, chunk)
             return inside
@@ -213,6 +283,8 @@
         one_step(STEPS - 1, even_post, odd_post)
 
     def last_inner(chunk, carry):
+        if relayed:
+            pass_on(None, last_post, STEPS, chunk)
         first = chunk * rows
         span = pl.ds(pl.multiple_of(first, 8), rows)
         streamed = {plane: stream_here(last_post, plane, first) for plane in inner}
@@ -229,6 +301,17 @@
         return carry
 
     lax.fori_loop(0, chunks, finish, 0)
+    if relayed:
+
+        @pl.when(me == RELAY)
+        def _():
+            def passed(k, carry):
+                _, from_up, _, from_down = relay_copies(last_post, k // chunks, k % chunks)
+                from_up.wait_send()
+                from_down.wait_send()
+                return carry
+
+            lax.fori_loop(0, STEPS * chunks, passed, 0)
 
 
 def last_kernel(rows, last_post, walls, stage, out, ends, inner_sem, out_sem):
@@ -283,6 +366,9 @@
         held_shape = (kinds, width + 2, depth + 2 * PAD, lanes)
         wall_shape = (3, width + 2, rows, lanes)
         hbm, vmem = pl.BlockSpec(memory_space=pltpu.HBM), pl.BlockSpec(memory_space=pltpu.VMEM)
+        relay = []
+        if n >= 8 and chunks > max(LAG_UP, LAG_DOWN):
+            relay = [pltpu.VMEM((STEPS, MOVING, depth, lanes), jnp.float32)] * 2 + [dma((STEPS, chunks))] * 4
         kept = pl.pallas_call(
             functools.partial(kernel, n, rows),
             out_shape=[
@@ -302,7 +388,7 @@
                 dma((STEPS, chunks)),
                 dma((STEPS, chunks)),
                 dma((4,)),
-            ],
+            ] + relay,
             compiler_params=pltpu.CompilerParams(
                 collective_id=0, has_side_effects=True, vmem_limit_bytes=55 * 1024 * 1024
             ),

time: 35.1 us -> 54.7 us (1.56)
  Pallas kernels: 34.9 us -> 54.5 us
    pallas_call x1, Pallas kernels: 33.3 us -> 52.9 us  [per_device(): pl.pallas_call(functools.partial(kernel, n, rows), out_shape=[pltpu.VMEM(...]
where the time goes in v4:
time: 54.7 us; the launch traced here: 54.5 us
  Pallas kernels  54.5 us (100%)
    pallas_call x1, Pallas kernels, per_device(): pl.pallas_call(functools.partial(kernel, n, rows), out_shape=[pltpu.VMEM(...  52.9 us
    pallas_call x1, Pallas kernels, per_device(): pl.pallas_call(functools.partial(last_kernel, rows), out_shape=jax.ShapeD...  1.61 us

profile of v4, /device:TPU:0, one launch (start us, length us, event | category | flops | bytes accessed | tf_op | source)
XLA Modules:
  0.0 54.5 jit_solution(13376246004346776321)
XLA Ops:
  0.0 52.9 %shard_map.28 = (f32[19,6,80,128]{3,2,1,0:T(8,128)S(1)}, s32[3,6,8,128]{3,2,1,0:T(8,128)S(1)}, f32[19,4,64,128]{3,2,1,0:T(8,128)S(1)}) custom-call(f32[19,4,64,128]{3,2,1,0:T(8,128)} %pops.1, s32[4,128]{1,0:T(4,128)} %heights.1), custom_call_target="tpu_custom_call" | custom-call | flops 49152000 | bytes 2490368 | tf_op jit(solution)/shard_map/pallas_call | solution.py:372
  52.9 1.6 %shard_map.29 = f32[19,4,64,128]{3,2,1,0:T(8,128)} custom-call(f32[19,6,80,128]{3,2,1,0:T(8,128)S(1)} %get-tuple-element.8.last_post, s32[3,6,8,128]{3,2,1,0:T(8,128)S(1)} %get-tuple-element.9.walls, f32[19,4,64,128]{3,2,1,0:T(8,128)S(1)} %get-tuple-element.10.stage), custom_call_target="tpu_custom_call" | custom-call | flops 12451840 | bytes 2490368 | tf_op jit(solution)/shard_map/pallas_call | solution.py:399

commit v5 on v2

--- a/solution.py
+++ b/solution.py
@@ -190,13 +190,21 @@
         def one_chunk(chunk, inside):
             first = chunk * rows
 
-            @pl.when(chunk < chunks - 1)
-            def _():
-                arrived(before, step - 1, chunk + 1)
-
-            keep_post(held, first, {plane: collide(stream_here(before, plane, first)) for plane in edges})
-            for copy in copies(held, step, chunk):
-                copy.start()
+            sides = ((1, 0, 1), (width, 1, 0))
+            for plane, needed, sent in sides:
+
+                @pl.when(chunk < chunks - 1)
+                def _():
+                    copies(before, step - 1, chunk + 1)[needed].wait_recv()
+                    if width == 1:
+                        copies(before, step - 1, chunk + 1)[1 - needed].wait_recv()
+
+                keep_post(held, first, {plane: collide(stream_here(before, plane, first))})
+                if width == 1:
+                    for copy in copies(held, step, chunk):
+                        copy.start()
+                    break
+                copies(held, step, chunk)[sent].start()
             keep_post(held, first, {plane: collide(stream_here(before, plane, first)) for plane in inner})
             left_here(before, step - 1, chunk)
             return inside

time: 35.1 us -> 35.8 us (1.020)
  Pallas kernels: 34.9 us -> 35.7 us
    pallas_call x1, Pallas kernels: 33.3 us -> 34 us  [per_device(): pl.pallas_call(functools.partial(kernel, n, rows), out_shape=[pltpu.VMEM(...]
where the time goes in v5:
time: 35.8 us; the launch traced here: 35.7 us
  Pallas kernels  35.7 us (100%)
    pallas_call x1, Pallas kernels, per_device(): pl.pallas_call(functools.partial(kernel, n, rows), out_shape=[pltpu.VMEM(...  34 us
    pallas_call x1, Pallas kernels, per_device(): pl.pallas_call(functools.partial(last_kernel, rows), out_shape=jax.ShapeD...  1.61 us

profile of v5, /device:TPU:0, one launch (start us, length us, event | category | flops | bytes accessed | tf_op | source)
XLA Modules:
  0.0 35.7 jit_solution(7650530851385731863)
XLA Ops:
  0.0 34.0 %shard_map.28 = (f32[19,6,80,128]{3,2,1,0:T(8,128)S(1)}, s32[3,6,8,128]{3,2,1,0:T(8,128)S(1)}, f32[19,4,64,128]{3,2,1,0:T(8,128)S(1)}) custom-call(f32[19,4,64,128]{3,2,1,0:T(8,128)} %pops.1, s32[4,128]{1,0:T(4,128)} %heights.1), custom_call_target="tpu_custom_call" | custom-call | flops 49152000 | bytes 2490368 | tf_op jit(solution)/shard_map/pallas_call | solution.py:294
  34.1 1.6 %shard_map.29 = f32[19,4,64,128]{3,2,1,0:T(8,128)} custom-call(f32[19,6,80,128]{3,2,1,0:T(8,128)S(1)} %get-tuple-element.8.last_post, s32[3,6,8,128]{3,2,1,0:T(8,128)S(1)} %get-tuple-element.9.walls, f32[19,4,64,128]{3,2,1,0:T(8,128)S(1)} %get-tuple-element.10.stage), custom_call_target="tpu_custom_call" | custom-call | flops 12451840 | bytes 2490368 | tf_op jit(solution)/shard_map/pallas_call | solution.py:321

commit v6 on v2

--- a/solution.py
+++ b/solution.py
@@ -242,8 +242,10 @@
     for copy in inner_copies:
         copy.start()
 
+    group = 4 if chunks % 4 == 0 else 1
+
     def write_back(chunk):
-        span = pl.ds(pl.multiple_of(chunk * rows, 8), rows)
+        span = pl.ds(pl.multiple_of((chunk - group + 1) * rows, 8), group * rows)
         return [
             pltpu.make_async_copy(ends.at[:, place, span], out.at[:, plane - 1, span], out_sem.at[chunk, place])
             for place, plane in enumerate(edges)
@@ -256,18 +258,22 @@
         for place, g in enumerate(streamed):
             for i in range(19):
                 ends[i, place, span, :] = g[i]
-        for copy in write_back(chunk):
-            copy.start()
+
+        @pl.when(chunk % group == group - 1)
+        def _():
+            for copy in write_back(chunk):
+                copy.start()
+
         return carry
 
     lax.fori_loop(0, chunks, one_chunk, 0)
 
     def finish(chunk, carry):
-        for copy in write_back(chunk):
+        for copy in write_back(chunk * group + group - 1):
             copy.wait()
         return carry
 
-    lax.fori_loop(0, chunks, finish, 0)
+    lax.fori_loop(0, chunks // group, finish, 0)
     for copy in inner_copies:
         copy.wait()
 

time: 35.1 us -> 35.2 us (level)
  no operation moved by 1% of the time
where the time goes in v6:
time: 35.2 us; the launch traced here: 35.1 us
  Pallas kernels  35.1 us (100%)
    pallas_call x1, Pallas kernels, per_device(): pl.pallas_call(functools.partial(kernel, n, rows), out_shape=[pltpu.VMEM(...  33.3 us
    pallas_call x1, Pallas kernels, per_device(): pl.pallas_call(functools.partial(last_kernel, rows), out_shape=jax.ShapeD...  1.74 us

profile of v6, /device:TPU:0, one launch (start us, length us, event | category | flops | bytes accessed | tf_op | source)
XLA Modules:
  0.0 35.1 jit_solution(8790207072088389659)
XLA Ops:
  0.0 33.3 %shard_map.28 = (f32[19,6,80,128]{3,2,1,0:T(8,128)S(1)}, s32[3,6,8,128]{3,2,1,0:T(8,128)S(1)}, f32[19,4,64,128]{3,2,1,0:T(8,128)S(1)}) custom-call(f32[19,4,64,128]{3,2,1,0:T(8,128)} %pops.1, s32[4,128]{1,0:T(4,128)} %heights.1), custom_call_target="tpu_custom_call" | custom-call | flops 49152000 | bytes 2490368 | tf_op jit(solution)/shard_map/pallas_call | solution.py:292
  33.3 1.7 %shard_map.29 = f32[19,4,64,128]{3,2,1,0:T(8,128)} custom-call(f32[19,6,80,128]{3,2,1,0:T(8,128)S(1)} %get-tuple-element.8.last_post, s32[3,6,8,128]{3,2,1,0:T(8,128)S(1)} %get-tuple-element.9.walls, f32[19,4,64,128]{3,2,1,0:T(8,128)S(1)} %get-tuple-element.10.stage), custom_call_target="tpu_custom_call" | custom-call | flops 12451840 | bytes 2490368 | tf_op jit(solution)/shard_map/pallas_call | solution.py:319
